TPU v7x, 512 devices: a whole 4x4x16 slice. The times are simulated.
512 devices in a mesh: stripe: 4 (over x), dp: 16 (over z_hi, y, core), tensor: 8 (over z_lo).
Axes of the slice: x: 4, y: 4, z: 16 (z_hi: 2, z_lo: 8; z = z_hi * 8 + z_lo), core: 2. Of those that a mesh axis runs over, the one named last changes fastest.
Arguments:
- normed_layer_input: bfloat16 [16384, 8192], P('dp', ('stripe', 'tensor')), may hold values from -6 to 6
- projection_output_gradient: bfloat16 [16384, 8192], P('dp', 'tensor'), may hold values from -6 to 6
- frozen_projection_weight: bfloat16 [8192, 8192], P('stripe', 'tensor'), may hold values from -0.0625 to 0.0625
- block_owner_tenant: int32 [128, 1], P('dp'), may hold values from 0 to 15
- block_token_fill: int32 [128, 1], P('dp'), may hold values from 32 to 128
- adapter_down_factors: bfloat16 [16, 48, 8192], P('dp', None, ('stripe', 'tensor')), may hold values from -0.0625 to 0.0625
- down_first_moment: float32 [16, 48, 8192], P('dp', None, ('stripe', 'tensor')), may hold values from -6 to 6
- down_second_moment: float32 [16, 48, 8192], P('dp', None, ('stripe', 'tensor')), may hold values from 1 to 100
- adapter_up_factors: bfloat16 [16, 16, 8192], P('dp', None, 'tensor'), may hold values from -0.119628906 to 0.119628906
- up_first_moment: float32 [16, 16, 8192], P('dp', None, 'tensor'), may hold values from -6 to 6
- up_second_moment: float32 [16, 16, 8192], P('dp', None, 'tensor'), may hold values from 1 to 100
Outputs:
- hidden_input_gradient: bfloat16 [16384, 8192], P('dp', ('stripe', 'tensor'))
- updated_down_factors: bfloat16 [16, 48, 8192], P('dp', None, ('stripe', 'tensor'))
- updated_down_first_moment: float32 [16, 48, 8192], P('dp', None, ('stripe', 'tensor'))
- updated_down_second_moment: float32 [16, 48, 8192], P('dp', None, ('stripe', 'tensor'))
- updated_up_factors: bfloat16 [16, 16, 8192], P('dp', None, 'tensor')
- updated_up_first_moment: float32 [16, 16, 8192], P('dp', None, 'tensor')
- updated_up_second_moment: float32 [16, 16, 8192], P('dp', None, 'tensor')
All inputs are finite; a program needn't handle non-finite values.
Results may differ from a plain program's by a relative error of at most 0.019.
Values may be sent and summed in bfloat16 or wider, within the bound.
A program may use at most 64 MiB of HBM per device.

v0:
```python
import jax
import jax.numpy as jnp
from jax import lax
from jax.sharding import PartitionSpec as P

HD = 128
QUERY_PER_GROUP = 6
ADAPTER_RANK = 16
BLK = 128


adapter_scale = 2.0
beta_one = 0.9
beta_two = 0.95
adam_rate = 0.001
adam_eps = 1e-08
adam_steps = 10.0


def section_backward(grad_heads, up_factor_heads, slot_count):
    queries = jnp.einsum(
        "btgph,brgph->btr",
        grad_heads[:, :, :, :slot_count],
        up_factor_heads[:, :, :, :slot_count],
        preferred_element_type=jnp.float32,
    )
    key_part = jnp.einsum(
        "btgh,brgh->btr",
        grad_heads[:, :, :, slot_count],
        up_factor_heads[:, :, :, slot_count],
        preferred_element_type=jnp.float32,
    )
    value_part = jnp.einsum(
        "btgh,brgh->btr",
        grad_heads[:, :, :, slot_count + 1],
        up_factor_heads[:, :, :, slot_count + 1],
        preferred_element_type=jnp.float32,
    )
    return jnp.concatenate([queries, key_part, value_part], axis=2)


def section_gradient(low_heads, grad_heads, slot_count):
    rank_size = low_heads.shape[2] // 3
    queries = jnp.einsum(
        "btr,btgph->brgph",
        low_heads[:, :, :rank_size],
        grad_heads[:, :, :, :slot_count],
        preferred_element_type=jnp.float32,
    )
    key_part = jnp.einsum(
        "btr,btgh->brgh",
        low_heads[:, :, rank_size : 2 * rank_size],
        grad_heads[:, :, :, slot_count],
        preferred_element_type=jnp.float32,
    )
    value_part = jnp.einsum(
        "btr,btgh->brgh",
        low_heads[:, :, 2 * rank_size :],
        grad_heads[:, :, :, slot_count + 1],
        preferred_element_type=jnp.float32,
    )
    joined = jnp.concatenate([queries, key_part[:, :, :, None], value_part[:, :, :, None]], axis=3)
    return joined.reshape(joined.shape[0], joined.shape[1], -1)


def apply_adam_update(params, moment, second, gradient):
    moment_new = beta_one * moment + (1.0 - beta_one) * gradient
    second_new = beta_two * second + (1.0 - beta_two) * (gradient * gradient)
    first_fix = moment_new / (1.0 - beta_one**adam_steps)
    second_fix = second_new / (1.0 - beta_two**adam_steps)
    stepped = params.astype(jnp.float32) - adam_rate * first_fix / (jnp.sqrt(second_fix) + adam_eps)
    return (stepped.astype(jnp.bfloat16), moment_new, second_new)


def on_device(
    normed_layer_input,
    projection_output_gradient,
    frozen_projection_weight,
    block_owner_tenant,
    block_token_fill,
    adapter_down_factors,
    down_first_moment,
    down_second_moment,
    adapter_up_factors,
    up_first_moment,
    up_second_moment,
):
    blocks = block_owner_tenant.shape[0]
    token_rows = projection_output_gradient.shape[0]
    width_portion = normed_layer_input.shape[1]
    col_part = projection_output_gradient.shape[1]
    heads_part = col_part // ((QUERY_PER_GROUP + 2) * HD)
    down_all, up_all = (
        lax.all_gather(adapter_down_factors, "dp", axis=0, tiled=True),
        lax.all_gather(adapter_up_factors, "dp", axis=0, tiled=True),
    )
    tenant_index = block_owner_tenant[:, 0]
    places = jnp.arange(BLK, dtype=jnp.int32)
    usable = places[None, :] < block_token_fill[:, 0][:, None]
    grad_blocks = projection_output_gradient.reshape(blocks, BLK, col_part)
    masked = jnp.where(usable[:, :, None], grad_blocks, jnp.zeros_like(grad_blocks))
    hid_blocks = normed_layer_input.reshape(blocks, BLK, width_portion)
    down_chosen_factor = down_all[tenant_index]
    up_chosen_factor = up_all[tenant_index]
    head_mask_rows = masked.reshape(blocks, BLK, heads_part, QUERY_PER_GROUP + 2, HD)
    up_factor_heads = up_chosen_factor.reshape(
        blocks, ADAPTER_RANK, heads_part, QUERY_PER_GROUP + 2, HD
    )
    low_part = jnp.einsum(
        "btd,brd->btr", hid_blocks, down_chosen_factor, preferred_element_type=jnp.float32
    )
    back_part = section_backward(head_mask_rows, up_factor_heads, QUERY_PER_GROUP)
    low_sum = lax.psum(low_part, ("stripe", "tensor"))
    backward_total = lax.psum(back_part, "tensor")
    backward_full = adapter_scale * backward_total
    base_part = lax.dot_general(
        masked.reshape(token_rows, col_part),
        frozen_projection_weight,
        (((1,), (1,)), ((), ())),
        preferred_element_type=jnp.float32,
    )
    frozen_total = lax.psum_scatter(
        base_part.astype(jnp.bfloat16), "tensor", scatter_dimension=1, tiled=True
    ).astype(jnp.float32)
    adapter_input = jnp.einsum(
        "lpm,lmw->lpw", backward_full, down_chosen_factor, preferred_element_type=jnp.float32
    )
    hidden_input_gradient = (
        frozen_total + adapter_input.reshape(token_rows, width_portion)
    ).astype(jnp.bfloat16)
    down_block = jnp.einsum(
        "btr,btd->brd", backward_full, hid_blocks, preferred_element_type=jnp.float32
    )
    up_factor_block = adapter_scale * section_gradient(low_sum, head_mask_rows, QUERY_PER_GROUP)
    owners = (
        tenant_index[:, None] == jnp.arange(down_all.shape[0], dtype=jnp.int32)[None, :]
    ).astype(jnp.float32)
    down_factor_gradient = jnp.einsum(
        "bn,brd->nrd", owners, down_block, precision=lax.Precision.HIGHEST
    )
    up_factor_gradient = jnp.einsum(
        "bn,brc->nrc", owners, up_factor_block, precision=lax.Precision.HIGHEST
    )
    down_gradient_total, up_gradient_total = lax.psum(
        (down_factor_gradient, up_factor_gradient), "dp"
    )
    token_offset = lax.axis_index("dp") * adapter_down_factors.shape[0]
    down_local_factor = lax.dynamic_slice_in_dim(
        down_gradient_total, token_offset, adapter_down_factors.shape[0], 0
    )
    up_local_factor = lax.dynamic_slice_in_dim(
        up_gradient_total, token_offset, adapter_up_factors.shape[0], 0
    )
    updated_down_factors, updated_down_first_moment, updated_down_second_moment = apply_adam_update(
        adapter_down_factors, down_first_moment, down_second_moment, down_local_factor
    )
    updated_up_factors, updated_up_first_moment, updated_up_second_moment = apply_adam_update(
        adapter_up_factors, up_first_moment, up_second_moment, up_local_factor
    )
    return (
        hidden_input_gradient,
        updated_down_factors,
        updated_down_first_moment,
        updated_down_second_moment,
        updated_up_factors,
        updated_up_first_moment,
        updated_up_second_moment,
    )


def solution(mesh):
    return jax.shard_map(
        on_device,
        mesh=mesh,
        in_specs=(
            P("dp", ("stripe", "tensor")),
            P("dp", "tensor"),
            P("stripe", "tensor"),
            P("dp", None),
            P("dp", None),
            P("dp", None, ("stripe", "tensor")),
            P("dp", None, ("stripe", "tensor")),
            P("dp", None, ("stripe", "tensor")),
            P("dp", None, "tensor"),
            P("dp", None, "tensor"),
            P("dp", None, "tensor"),
        ),
        out_specs=(
            P("dp", ("stripe", "tensor")),
            P("dp", None, ("stripe", "tensor")),
            P("dp", None, ("stripe", "tensor")),
            P("dp", None, ("stripe", "tensor")),
            P("dp", None, "tensor"),
            P("dp", None, "tensor"),
            P("dp", None, "tensor"),
        ),
        check_vma=False,
    )
```

profile of v0, /device:TPU:1, one launch (start us, length us, event | category | flops | bytes accessed | tf_op | source)
XLA Modules:
  0.0 716.7 jit_solution(18085544395107876769)
XLA Ops:
  7.2 0.7 fusion.26
  7.9 0.7 fusion.30
  8.7 52.7 %all_gather.6 = bf16[16,16,1024]{2,1,0:T(8,128)(2,1)S(1)} all-gather(bf16[1,16,1024]{2,1,0:T(8,128)(2,1)} %param.19), channel_id=1, replica_groups=mesh['stripe'=4,'dp'=16,'tensor'=8] {'dp'}, dimensions={0}, use_global_device_ids=true | all-gather | bytes 557056 | tf_op jit(solution)/shard_map/all_gather | solution.py:95
  61.4 0.6 gather_fusion
  62.1 2.2 copy.95
  64.4 0.3 copy_select_fusion
  64.7 0.5 fusion.5
  65.7 0.7 pad_maximum_fusion
  66.5 35.8 %all_gather.7 = bf16[16,48,256]{2,1,0:T(8,128)(2,1)S(1)} all-gather(bf16[1,48,256]{2,1,0:T(8,128)(2,1)S(1)} %copy-done.4), channel_id=1, replica_groups=mesh['stripe'=4,'dp'=16,'tensor'=8] {'dp'}, dimensions={0}, use_global_device_ids=true | all-gather | bytes 417792 | tf_op jit(solution)/shard_map/all_gather | solution.py:94
  102.3 0.6 gather_fusion.1
  103.2 205.1 %all-reduce.8 = bf16[8,128,48]{1,2,0:T(8,128)(2,1)S(1)} all-reduce(f32[8,128,48]{1,2,0:T(8,128)S(1)} %convolution_bitcast_fusion), channel_id=1, replica_groups=mesh['stripe'=4,'dp'=16,'tensor'=8] {'stripe','tensor'}, use_global_device_ids=true, to_apply=%region_3.4 | all-reduce | flops 49152 | bytes 294912 | tf_op jit(solution)/shard_map/psum | solution.py:113
  309.3 0.7 fusion.21
  310.0 1.6 copy.87
  311.6 1.1 fusion.12
  312.8 0.7 fusion.8
  313.5 1.3 copy.84
  314.9 8.5 %convolution_convert_fusion = bf16[1024,2048]{1,0:T(8,128)(2,1)} fusion(bf16[2048,1024]{1,0:T(8,128)(2,1)} %param.13, bf16[1024,1024]{1,0:T(8,128)(2,1)S(1)} %copy-done.1, pred[1024]{0:T(1024)(128)(4,1)S(1)} %get-tuple-element.38), kind=kOutput, calls=%fused_computation.2 | convolution fusion | flops 4298113024 | bytes 10486784 | tf_op jit(solution)/shard_map/dot_general | solution.py:116
  323.5 0.9 copy-done.2
  324.4 0.3 fusion.14
  324.7 275.1 %all-reduce.7.cloned.1.call-done = (f32[16,48,256]{2,1,0:T(8,128)}, f32[16,16,1024]{2,1,0:T(8,128)}) async-done(((f32[16,48,256]{2,1,0:T(8,128)}, f32[16,16,1024]{2,1,0:T(8,128)}), (f32[16,48,256]{2,1,0:T(8,128)}, f32[16,16,1024]{2,1,0:T(8,128)})) %all-reduce.7.cloned.1.call-update) | async-done | bytes 1835024 | tf_op jit(solution)/shard_map/psum | solution.py:144
  599.8 1.5 subtract_convert_fusion.1
  601.3 1.5 subtract_convert_fusion
  602.8 105.3 %reduce-scatter.2.cloned.1.call-done = bf16[1024,256]{1,0:T(8,128)(2,1)} async-done(((bf16[1024,2048]{1,0:T(8,128)(2,1)}), bf16[1024,256]{1,0:T(8,128)(2,1)}) %reduce-scatter.2.cloned.1.call-update) | async-done | bytes 524304 | tf_op jit(solution)/shard_map/reduce_scatter | solution.py:122
  708.1 2.1 fusion.6
  (38 shorter events, 2.2 us)
Async XLA Ops:
  7.2 95.7 %copy-start = (bf16[1024,256]{1,0:T(8,128)(2,1)S(1)}, bf16[1024,256]{1,0:T(8,128)(2,1)}, u32[]{:S(2)}) copy-start(bf16[1024,256]{1,0:T(8,128)(2,1)} %param.11) | copy-start | bytes 1572868
  7.2 304.5 %all-reduce.5.cloned.1.call-start = ((), (), s32[]{:S(2)}) async-start(), calls=%async_computation.2 | async-start | bytes 393216 | tf_op jit(solution)/shard_map/psum | solution.py:114
  64.7 1.8 copy-start.4
  66.5 533.3 %all-reduce.7.cloned.1.call-start = ((), (), s32[]{:S(2)}) async-start(), calls=%async_computation.3 | async-start | bytes 3670016 | tf_op jit(solution)/shard_map/psum | solution.py:144
  308.7 0.7 copy-start.9
  312.8 2.1 copy-start.1
  314.9 393.3 %reduce-scatter.2.cloned.1.call-start = ((), (), s32[]{:S(2)}) async-start(), calls=%async_computation.1 | async-start | bytes 4718592 | tf_op jit(solution)/shard_map/reduce_scatter | solution.py:122
  323.5 0.9 copy-start.2
  323.5 276.3 %copy-start.7 = (f32[1,48,256]{2,1,0:T(8,128)S(1)}, f32[1,48,256]{2,1,0:T(8,128)}, u32[]{:S(2)}) copy-start(f32[1,48,256]{2,1,0:T(8,128)} %param.17) | copy-start | bytes 147460
  323.5 276.3 %copy-start.8 = (f32[1,48,256]{2,1,0:T(8,128)S(1)}, f32[1,48,256]{2,1,0:T(8,128)}, u32[]{:S(2)}) copy-start(f32[1,48,256]{2,1,0:T(8,128)} %param.18) | copy-start | bytes 147460
  323.5 277.8 %copy-start.3 = (bf16[1,16,1024]{2,1,0:T(8,128)(2,1)S(1)}, bf16[1,16,1024]{2,1,0:T(8,128)(2,1)}, u32[]{:S(2)}) copy-start(bf16[1,16,1024]{2,1,0:T(8,128)(2,1)} %param.19) | copy-start | bytes 98308
  323.5 277.8 %copy-start.5 = (f32[1,16,1024]{2,1,0:T(8,128)S(1)}, f32[1,16,1024]{2,1,0:T(8,128)}, u32[]{:S(2)}) copy-start(f32[1,16,1024]{2,1,0:T(8,128)} %param.20) | copy-start | bytes 196612
  323.5 277.8 %copy-start.6 = (f32[1,16,1024]{2,1,0:T(8,128)S(1)}, f32[1,16,1024]{2,1,0:T(8,128)}, u32[]{:S(2)}) copy-start(f32[1,16,1024]{2,1,0:T(8,128)} %param.21) | copy-start | bytes 196612
Sparse Core Ops, SparseCore 0:
  66.6 107.5 all-reduce.4
  315.0 284.7 all-reduce.6
  602.6 105.4 reduce-scatter.1
where the time goes:
time: 717 us
  waiting for transfers between devices  380 us (53%)
  blocking collectives  294 us (41%)
  between operations  13.9 us (2%)
  matrix products  13.4 us (2%)
  local copies, waits for them, and re-layouts  7.63 us (1%)
  other arithmetic  7.56 us (1%)
    psum x1, waiting for transfers between devices, on_device(): lax.psum((down_factor_gradient, up_factor_gradient), 'dp')  275 us
    psum x1, blocking collectives, on_device(): low_sum = lax.psum(low_part, ('stripe', 'tensor'))  205 us
    reduce_scatter x1, waiting for transfers between devices, on_device(): lax.psum_scatter(base_part.astype(jnp.bfloat16), 'tensor', scatter_dimens...  105 us
    all_gather x1, blocking collectives, on_device(): lax.all_gather(adapter_up_factors, 'dp', axis=0, tiled=True)  52.7 us
    all_gather x1, blocking collectives, on_device(): lax.all_gather(adapter_down_factors, 'dp', axis=0, tiled=True)  35.8 us
  transfers between devices with their start and end apart: 3, of which 2 were waited for; matrix products, arithmetic and copies ran while one was open for 2% of the time, Pallas kernels for 0%

commit v1 on v0

v1 whole, which is shorter than its diff:
```python
import functools

import jax
import jax.numpy as jnp
from jax import lax
from jax.experimental import pallas as pl
from jax.experimental.pallas import tpu as pltpu
from jax.sharding import PartitionSpec as P

BLK = 128
RANK = 16
DOWN = 48
FAC = 64
PIECES = 4
SKEW = 2
AHEAD = 2

adapter_scale = 2.0
beta_one = 0.9
beta_two = 0.95
adam_rate = 0.001
adam_eps = 1e-08
adam_steps = 10.0

F32 = jnp.float32
BF16 = jnp.bfloat16
MESH = pl.DeviceIdType.MESH

AT_FORWARD = 1
AT_PROJECT = 3
AT_STRIPE_SUM = 5
AT_TENSOR_SUM = 6
AT_STRIPE_SPREAD = 8
AT_GRADIENT = 9
AT_GROUP_SUM = 12
AT_HALF_SUM = 15
AT_UP_ADAM = 17


def adam(params, moment, second, gradient):
    moment_new = beta_one * moment + (1.0 - beta_one) * gradient
    second_new = beta_two * second + (1.0 - beta_two) * (gradient * gradient)
    first_fix = moment_new / (1.0 - beta_one**adam_steps)
    second_fix = second_new / (1.0 - beta_two**adam_steps)
    stepped = params.astype(F32) - adam_rate * first_fix / (jnp.sqrt(second_fix) + adam_eps)
    return stepped.astype(BF16), moment_new, second_new


def kernel(
    S, NP, NT,
    ten_ref, fill_ref,
    x_in, a_in, w_in, dn_in, dm_in, dv_in, up_in, um_in, uv_in,
    out_o, dn_o, dm_o, dv_o, up_o, um_o, uv_o,
    av, wv, xv, fac, pv, rv,
    lp, xrs, xs, zrs, lb,
    gl, ul, gp, grs, go, gs, gz, ux, acc, ov,
    dmv, dvv, umv, uvv, upv, dnn, upn,
    load_sem, w_sem, out_sem, store_sem,
    line_send, line_recv,
    fac_send, fac_recv,
    xr_send, xr_recv, zr_send, zr_recv, za_send, za_recv, xa_send, xa_recv,
    gr_send, gr_recv, gz_send, gz_recv, ux_send, ux_recv,
):
    G = NP // 2
    TOK, C = av.shape
    D = xv.shape[1]
    NB = TOK // BLK
    QT = TOK // S
    CQ = C // S
    HALF = CQ // 2
    PR = TOK // PIECES
    CHUNK = wv.shape[0] // NT
    s = lax.axis_index("stripe")
    p = lax.axis_index("dp")
    t = lax.axis_index("tensor")
    zh = lax.div(p, G)
    m = lax.rem(p, G)
    pz = (1 - zh) * G + m

    def other(axis, here, size, o):
        return {axis: lax.rem(here + o, size)}

    def group_peer(o):
        return zh * G + lax.rem(m + o, G)

    quarter = pl.ds(pl.multiple_of(s * CQ, CQ), CQ)
    my_tokens = pl.ds(pl.multiple_of(s * QT, QT), QT)
    loads = [
        pltpu.make_async_copy(dn_in.at[0], fac.at[p, pl.ds(0, DOWN)], load_sem.at[0]),
        pltpu.make_async_copy(up_in.at[0, :, quarter], fac.at[p, pl.ds(DOWN, RANK)], load_sem.at[1]),
        pltpu.make_async_copy(a_in, av, load_sem.at[2]),
        pltpu.make_async_copy(x_in, xv, load_sem.at[3]),
        pltpu.make_async_copy(dm_in.at[0], dmv, load_sem.at[4]),
        pltpu.make_async_copy(dv_in.at[0], dvv, load_sem.at[5]),
        pltpu.make_async_copy(um_in.at[0], umv, load_sem.at[6]),
        pltpu.make_async_copy(uv_in.at[0], uvv, load_sem.at[7]),
        pltpu.make_async_copy(up_in.at[0], upv, load_sem.at[8]),
    ]

    def order(i):
        inner = jnp.where(lax.rem(i, 2) == 0, NT - 1 - lax.div(i, 2), lax.div(i, 2))
        return jnp.where(t == 0, NT - 1 - i, jnp.where(t == NT - 1, i, inner))

    def w_load(j):
        rows = pl.ds(pl.multiple_of(j * CHUNK, CHUNK), CHUNK)
        return pltpu.make_async_copy(w_in.at[rows], wv.at[rows], w_sem.at[j])

    for load in loads[:3]:
        load.start()
    for i in range(NT):
        w_load(order(jnp.int32(i))).start()
    for load in loads[3:]:
        load.start()

    barrier = pltpu.get_barrier_semaphore()
    partners = [other("tensor", t, NT, o) for o in range(1, NT)]
    partners += [other("stripe", s, S, o) for o in range(1, S)]
    partners += [{"dp": group_peer(o)} for o in range(1, G)]
    partners += [{"dp": pz}]
    for partner in partners:
        pl.semaphore_signal(barrier, inc=1, device_id=partner, device_id_type=MESH)

    loads[2].wait()

    @pl.loop(0, NB)
    def _(b):
        rows = pl.ds(pl.multiple_of(b * BLK, BLK), BLK)
        place = lax.broadcasted_iota(jnp.int32, (BLK, C), 0)
        block = av[rows, :]
        av[rows, :] = jnp.where(place < fill_ref[b, 0], block, jnp.zeros_like(block))

    loads[0].wait()
    loads[1].wait()
    pl.semaphore_wait(barrier, len(partners))

    def remote(src, dst, send, recv, device):
        return pltpu.make_async_remote_copy(
            src_ref=src, dst_ref=dst, send_sem=send, recv_sem=recv, device_id=device, device_id_type=MESH
        )

    def fac_copy(slot, i, device):
        return remote(fac.at[slot], fac.at[slot], fac_send.at[i], fac_recv.at[slot], device)

    def xr_copy(o):
        to = lax.rem(s + o, S)
        lanes = pl.ds(pl.multiple_of(to * QT, QT), QT)
        return remote(lp.at[:, lanes], xrs.at[s], xr_send.at[o], xr_recv.at[s], {"stripe": to})

    def owner(g):
        return (g + 1) % NT

    def section(g):
        return pl.ds(g * RANK, RANK)

    def zr_copy(g):
        return remote(xs.at[section(g)], zrs.at[g, t], zr_send.at[g], zr_recv.at[g, t], {"tensor": owner(g)})

    def za_copy(g, o):
        part = lb.at[section(g), my_tokens]
        return remote(part, part, za_send.at[g, o], za_recv.at[g], other("tensor", t, NT, o))

    def xa_copy(o):
        part = lb.at[:, my_tokens]
        return remote(part, part, xa_send.at[o], xa_recv.at[s], other("stripe", s, S, o))

    def gr_copy(o):
        to = lax.rem(m + o, G)
        return remote(gp.at[to], grs.at[m], gr_send.at[o], gr_recv.at[m], {"dp": zh * G + to})

    def gz_copy():
        return remote(gs, gz, gz_send, gz_recv, {"dp": pz})

    def ux_copy(o):
        return remote(ux.at[s], ux.at[s], ux_send.at[o], ux_recv.at[s], other("stripe", s, S, o))

    fac_copy(p, 0, {"dp": pz}).start()
    for o in range(1, G):
        fac_copy(p, o, {"dp": group_peer(o)}).start()

    def forward():
        fac_copy(pz, 0, {"dp": pz}).wait_recv()
        for o in range(1, G):
            fac_copy(pz, G + o, {"dp": group_peer(o)}).start()

    def project():
        for o in range(1, G):
            fac_copy(zh * G + lax.rem(m + o, G), 0, {"dp": pz}).wait_recv()
            fac_copy((1 - zh) * G + lax.rem(m + o, G), 0, {"dp": pz}).wait_recv()
        loads[3].wait()
        last = s == S - 1
        zero = jnp.zeros((RANK, BLK), F32)

        @pl.loop(0, NB)
        def _(b):
            rows = pl.ds(pl.multiple_of(b * BLK, BLK), BLK)
            chosen = fac[ten_ref[b, 0]]
            nt = (((1,), (1,)), ((), ()))
            low = lax.dot_general(chosen[:DOWN], xv[rows, :], nt, preferred_element_type=F32)
            grad = av[rows, quarter]
            first = lax.dot_general(chosen[DOWN:, :HALF], grad[:, :HALF], nt, preferred_element_type=F32)
            second = lax.dot_general(chosen[DOWN:, HALF:], grad[:, HALF:], nt, preferred_element_type=F32)
            both = jnp.concatenate(
                [
                    low,
                    jnp.where(last, zero, first + second),
                    jnp.where(last, first, zero),
                    jnp.where(last, second, zero),
                ],
                axis=0,
            )
            lp[:, rows] = (adapter_scale * both).astype(BF16)

        for o in range(1, S):
            xr_copy(o).start()

    def stripe_sum():
        total = lp[:, my_tokens].astype(F32)
        for o in range(1, S):
            src = lax.rem(s + o, S)
            remote(xs, xrs.at[src], xr_send.at[0], xr_recv.at[src], {"dp": pz}).wait_recv()
            total += xrs[src].astype(F32)
        xs[...] = total.astype(BF16)
        for g in range(6):

            @pl.when(t != owner(g))
            def _(g=g):
                zr_copy(g).start()

    def tensor_sum():
        for g in range(6):

            @pl.when(t == owner(g))
            def _(g=g):
                def add(o, total):
                    src = lax.rem(t + o, NT)
                    remote(
                        xs.at[section(g)], zrs.at[g, src], zr_send.at[g], zr_recv.at[g, src], {"dp": pz}
                    ).wait_recv()
                    return total + zrs[g, src].astype(F32)

                total = lax.fori_loop(1, NT, add, xs[section(g), :].astype(F32))
                lb[section(g), my_tokens] = total.astype(BF16)
                for o in range(1, NT):
                    za_copy(g, o).start()

    def stripe_spread():
        for g in range(6):

            @pl.when(t != owner(g))
            def _(g=g):
                za_copy(g, 1).wait_recv()

        for o in range(1, S):
            xa_copy(o).start()

    group = min(4, NP)

    def gradient():
        for o in range(1, S):
            src = lax.rem(s + o, S)
            part = lb.at[:, pl.ds(pl.multiple_of(src * QT, QT), QT)]
            remote(part, part, xa_send.at[0], xa_recv.at[src], {"dp": pz}).wait_recv()
        block_of = lax.div(lax.broadcasted_iota(jnp.int32, (1, TOK), 1), BLK)
        tenant = jnp.zeros((1, TOK), jnp.int32)
        for b in range(NB):
            tenant = jnp.where(block_of == b, ten_ref[b, 0], tenant)
        last = s == S - 1
        sec_first = jnp.where(last, RANK, 0)
        sec_second = jnp.where(last, 2 * RANK, 0)

        @pl.loop(0, NP)
        def _(n):
            here = jnp.where(tenant == n, 1.0, 0.0).astype(BF16)
            gl[pl.ds(pl.multiple_of(n * DOWN, RANK), DOWN), :] = lb[pl.ds(DOWN, DOWN), :] * here
            rows = pl.ds(pl.multiple_of(n * RANK, RANK), RANK)
            ul[0, rows, :] = lb[pl.ds(pl.multiple_of(sec_first, RANK), RANK), :] * here
            ul[1, rows, :] = lb[pl.ds(pl.multiple_of(sec_second, RANK), RANK), :] * here

        @pl.loop(0, NP // group)
        def _(i):
            rows = pl.ds(pl.multiple_of(i * group * DOWN, RANK), group * DOWN)
            part = jnp.dot(gl[rows, :], xv[...], preferred_element_type=F32).astype(BF16)
            for e in range(group):
                n = i * group + e
                gp[lax.rem(n, G), lax.div(n, G), :DOWN, :] = part[e * DOWN : (e + 1) * DOWN]

        for h in range(2):
            lanes = pl.ds(pl.multiple_of(s * CQ + h * HALF, HALF), HALF)
            part = jnp.dot(ul[h], av[:, lanes], preferred_element_type=F32).astype(BF16)
            for n in range(NP):
                gp[n % G, n // G, DOWN:, h * HALF : (h + 1) * HALF] = part[n * RANK : (n + 1) * RANK]

        for o in range(1, G):
            gr_copy(o).start()

        @pl.loop(0, NB)
        def _(b):
            rows = pl.ds(pl.multiple_of(b * BLK, BLK), BLK)
            down = fac[ten_ref[b, 0]][:DOWN]
            extra = lax.dot_general(
                lb[pl.ds(DOWN, DOWN), rows], down, (((0,), (0,)), ((), ())), preferred_element_type=F32
            )
            acc[rows, :] = extra + pv[t, rows, :].astype(F32)

    def group_sum():
        for o in range(1, G):
            src = lax.rem(m + o, G)
            remote(gp.at[0], grs.at[src], gr_send.at[0], gr_recv.at[src], {"dp": pz}).wait_recv()

        def total(half):
            value = gp[m, half].astype(F32)
            for o in range(1, G):
                value += grs[lax.rem(m + o, G), half].astype(F32)
            return value

        gs[...] = total(1 - zh).astype(BF16)
        gz_copy().start()
        go[...] = total(zh)

    def half_sum():
        gz_copy().wait_recv()
        grad = go[...] + gz[...].astype(F32)
        ux[s] = grad[DOWN:]
        for o in range(1, S):
            ux_copy(o).start()
        for load in loads[4:]:
            load.wait()
        dnn[...], dmv[...], dvv[...] = adam(fac[p, :DOWN, :], dmv[...], dvv[...], grad[:DOWN])
        for store in stores[:3]:
            store.start()

    def up_adam():
        for o in range(1, S):
            src = lax.rem(s + o, S)
            remote(ux.at[src], ux.at[src], ux_send.at[0], ux_recv.at[src], {"dp": pz}).wait_recv()
        for i in range(S):
            lanes = pl.ds(i * CQ, CQ)
            upn[:, lanes], umv[:, lanes], uvv[:, lanes] = adam(
                upv[:, lanes], umv[:, lanes], uvv[:, lanes], ux[i]
            )
        for store in stores[3:]:
            store.start()

    stores = [
        pltpu.make_async_copy(dnn, dn_o.at[0], store_sem.at[0]),
        pltpu.make_async_copy(dmv, dm_o.at[0], store_sem.at[1]),
        pltpu.make_async_copy(dvv, dv_o.at[0], store_sem.at[2]),
        pltpu.make_async_copy(upn, up_o.at[0], store_sem.at[3]),
        pltpu.make_async_copy(umv, um_o.at[0], store_sem.at[4]),
        pltpu.make_async_copy(uvv, uv_o.at[0], store_sem.at[5]),
    ]

    def multiply(i):
        j = order(i)
        w_load(j).wait()

        @pl.loop(0, PIECES)
        def _(q):
            rows = pl.ds(pl.multiple_of(q * PR, PR), PR)
            part = lax.dot_general(
                av[rows, :],
                wv[pl.ds(pl.multiple_of(j * CHUNK, CHUNK), CHUNK), :],
                (((1,), (1,)), ((), ())),
                preferred_element_type=F32,
            )
            pv[j, rows, :] = part.astype(BF16)

    def rank(way):
        return t if way == 0 else NT - 1 - t

    def line_copy(way, u):
        k, q = lax.div(u, PIECES), lax.rem(u, PIECES)
        j = NT - 1 - k if way == 0 else k
        rows = pl.ds(pl.multiple_of(q * PR, PR), PR)
        to = t + 1 if way == 0 else t - 1
        return j, rows, remote(
            pv.at[j, rows], rv.at[way, j, rows], line_send.at[j, q], line_recv.at[way, j, q], {"tensor": to}
        )

    def line_step(v):
        for way in range(2):
            r = rank(way)
            u = v - SKEW * r

            @pl.when((u >= 0) & (u < (NT - 1 - r) * PIECES))
            def _(way=way, r=r, u=u):
                j, rows, copy = line_copy(way, u)

                @pl.when(r > 0)
                def _():
                    copy.wait_recv()
                    pv[j, rows, :] = (pv[j, rows, :].astype(F32) + rv[way, j, rows, :].astype(F32)).astype(BF16)

                @pl.when(u >= AHEAD)
                def _():
                    line_copy(way, u - AHEAD)[2].wait_send()

                copy.start()

    stages = [
        (AT_FORWARD, forward),
        (AT_PROJECT, project),
        (AT_STRIPE_SUM, stripe_sum),
        (AT_TENSOR_SUM, tensor_sum),
        (AT_STRIPE_SPREAD, stripe_spread),
        (AT_GRADIENT, gradient),
        (AT_GROUP_SUM, group_sum),
        (AT_HALF_SUM, half_sum),
        (AT_UP_ADAM, up_adam),
    ]
    steps = max((NT - 1 - r) * PIECES + SKEW * r for r in range(NT - 1))
    steps = max(steps, AT_UP_ADAM + 1, NT)

    @pl.loop(0, steps)
    def _(v):
        @pl.when(v < NT)
        def _():
            multiply(v)

        line_step(v)
        for at, stage in stages:
            pl.when(v == at)(stage)

    def finish(q):
        rows = pl.ds(q * PR, PR)
        for way in range(2):

            @pl.when(rank(way) > 0)
            def _(way=way):
                part = rv.at[way, t, rows]
                remote(part, part, line_send.at[t, q], line_recv.at[way, t, q], {"dp": pz}).wait_recv()
                acc[rows, :] += rv[way, t, rows, :].astype(F32)

        ov[rows, :] = acc[rows, :].astype(BF16)
        return pltpu.make_async_copy(ov.at[rows], out_o.at[rows], out_sem.at[q])

    writes = []
    for q in range(PIECES):
        write = finish(q)
        write.start()
        writes.append(write)

    for way in range(2):
        r = rank(way)

        @pl.when(r < NT - 1)
        def _(way=way, r=r):
            for back in range(AHEAD):
                line_copy(way, (NT - 1 - r) * PIECES - AHEAD + back)[2].wait_send()

    fac_copy(p, 0, {"dp": pz}).wait_send()
    for o in range(1, G):
        fac_copy(p, o, {"dp": group_peer(o)}).wait_send()
        fac_copy(pz, G + o, {"dp": group_peer(o)}).wait_send()
        gr_copy(o).wait_send()
    for o in range(1, S):
        xr_copy(o).wait_send()
        xa_copy(o).wait_send()
        ux_copy(o).wait_send()
    for g in range(6):

        @pl.when(t != owner(g))
        def _(g=g):
            zr_copy(g).wait_send()

        @pl.when(t == owner(g))
        def _(g=g):
            for o in range(1, NT):
                za_copy(g, o).wait_send()

    gz_copy().wait_send()
    for store in stores:
        store.wait()
    for write in writes:
        write.wait()


def on_device(
    S, NP, NT,
    normed_layer_input,
    projection_output_gradient,
    frozen_projection_weight,
    block_owner_tenant,
    block_token_fill,
    adapter_down_factors,
    down_first_moment,
    down_second_moment,
    adapter_up_factors,
    up_first_moment,
    up_second_moment,
):
    tok, d = normed_layer_input.shape
    c = projection_output_gradient.shape[1]
    w_rows = frozen_projection_weight.shape[0]
    G = NP // 2
    qt = tok // S
    any_space = pl.BlockSpec(memory_space=pl.ANY)
    smem = pl.BlockSpec(memory_space=pltpu.SMEM)
    outs = (
        jax.ShapeDtypeStruct((tok, d), BF16),
        jax.ShapeDtypeStruct(adapter_down_factors.shape, BF16),
        jax.ShapeDtypeStruct(down_first_moment.shape, F32),
        jax.ShapeDtypeStruct(down_second_moment.shape, F32),
        jax.ShapeDtypeStruct(adapter_up_factors.shape, BF16),
        jax.ShapeDtypeStruct(up_first_moment.shape, F32),
        jax.ShapeDtypeStruct(up_second_moment.shape, F32),
    )
    vm, dma = pltpu.VMEM, pltpu.SemaphoreType.DMA
    scratch = [
        vm((tok, c), BF16),
        vm((w_rows, c), BF16),
        vm((tok, d), BF16),
        vm((NP, FAC, d), BF16),
        vm((NT, tok, w_rows // NT), BF16),
        vm((2, NT, tok, w_rows // NT), BF16),
        vm((2 * DOWN, tok), BF16),
        vm((S, 2 * DOWN, qt), BF16),
        vm((2 * DOWN, qt), BF16),
        vm((6, NT, RANK, qt), BF16),
        vm((2 * DOWN, tok), BF16),
        vm((NP * DOWN, tok), BF16),
        vm((2, NP * RANK, tok), BF16),
        vm((G, 2, FAC, d), BF16),
        vm((G, 2, FAC, d), BF16),
        vm((FAC, d), F32),
        vm((FAC, d), BF16),
        vm((FAC, d), BF16),
        vm((S, RANK, c // S), F32),
        vm((tok, d), F32),
        vm((tok, d), BF16),
        vm((DOWN, d), F32),
        vm((DOWN, d), F32),
        vm((RANK, c), F32),
        vm((RANK, c), F32),
        vm((RANK, c), BF16),
        vm((DOWN, d), BF16),
        vm((RANK, c), BF16),
        dma((9,)), dma((NT,)), dma((PIECES,)), dma((6,)),
        dma((NT, PIECES)), dma((2, NT, PIECES)),
        dma((2 * G,)), dma((NP,)),
        dma((S,)), dma((S,)), dma((6,)), dma((6, NT)), dma((6, NT)), dma((6,)), dma((S,)), dma((S,)),
        dma((G,)), dma((G,)), dma, dma, dma((S,)), dma((S,)),
    ]
    return pl.pallas_call(
        functools.partial(kernel, S, NP, NT),
        out_shape=outs,
        in_specs=[smem] * 2 + [any_space] * 9,
        out_specs=[any_space] * 7,
        scratch_shapes=scratch,
        compiler_params=pltpu.CompilerParams(
            collective_id=0, has_side_effects=True, vmem_limit_bytes=48 * 1024 * 1024
        ),
        cost_estimate=pl.CostEstimate(
            flops=2 * tok * c * w_rows, bytes_accessed=2 * (tok * c + w_rows * c), transcendentals=0
        ),
        name="united_backward",
    )(
        block_owner_tenant,
        block_token_fill,
        normed_layer_input,
        projection_output_gradient,
        frozen_projection_weight,
        adapter_down_factors,
        down_first_moment,
        down_second_moment,
        adapter_up_factors,
        up_first_moment,
        up_second_moment,
    )


def solution(mesh):
    both = ("stripe", "tensor")
    return jax.shard_map(
        functools.partial(on_device, mesh.shape["stripe"], mesh.shape["dp"], mesh.shape["tensor"]),
        mesh=mesh,
        in_specs=(
            P("dp", both),
            P("dp", "tensor"),
            P("stripe", "tensor"),
            P("dp", None),
            P("dp", None),
            P("dp", None, both),
            P("dp", None, both),
            P("dp", None, both),
            P("dp", None, "tensor"),
            P("dp", None, "tensor"),
            P("dp", None, "tensor"),
        ),
        out_specs=(
            P("dp", both),
            P("dp", None, both),
            P("dp", None, both),
            P("dp", None, both),
            P("dp", None, "tensor"),
            P("dp", None, "tensor"),
            P("dp", None, "tensor"),
        ),
        check_vma=False,
    )
```

time: 717 us -> 126 us (0.18)
  the two profiles are of different devices: /device:TPU:1 before, /device:TPU:32 now
where the time goes in v1:
time: 126 us
  Pallas kernels  112 us (89%)
  local copies, waits for them, and re-layouts  13.4 us (11%)
    pallas_call x1, Pallas kernels, on_device(): pl.pallas_call(functools.partial(kernel, S, NP, NT), out_shape=outs, in_s...  112 us
    unnamed x25, local copies, waits for them, and re-layouts  13.4 us

profile of v1, /device:TPU:32, one launch (start us, length us, event | category | flops | bytes accessed | tf_op | source)
XLA Modules:
  0.0 125.9 jit_solution(3104782973129060642)
XLA Ops:
  0.6 0.7 copy.18.ten_ref
  1.4 0.7 copy.19.fill_ref
  2.1 0.0 copy-start
  2.1 1.6 %copy-done = bf16[1024,1024]{1,0:T(8,128)(2,1)S(1)} copy-done((bf16[1024,1024]{1,0:T(8,128)(2,1)S(1)}, bf16[1024,1024]{1,0:T(8,128)(2,1)}, u32[]{:S(2)}) %copy-start) | copy-done | bytes 2097176
  3.7 0.0 copy-start.1
  3.7 1.0 copy-done.1
  4.7 0.0 copy-start.2
  4.7 0.8 copy-done.2
  5.6 0.0 copy-start.3
  5.6 0.8 copy-done.3
  6.4 0.0 copy-start.4
  6.4 0.8 copy-done.4
  7.2 0.0 copy-start.5
  7.2 0.8 copy-done.5
  8.0 0.8 copy-done.6
  8.8 0.7 copy-done.7
  9.5 111.9 %united_backward.1 = (bf16[1024,256]{1,0:T(8,128)(2,1)S(1)}, bf16[1,48,256]{2,1,0:T(8,128)(2,1)S(1)}, f32[1,48,256]{2,1,0:T(8,128)S(1)}, f32[1,48,256]{2,1,0:T(8...) custom-call(s32[8,1]{1,0:T(8,128)S(1)} %copy.18.ten_ref, ...), custom_call_target="tpu_custom_call" | custom-call | flops 4294967296 | bytes 6291456 | tf_op jit(solution)/shard_map/united_backward/pallas_call | solution.py:544
  121.4 0.8 copy.27
  122.2 0.6 copy.28
  122.8 0.6 copy.29
  123.4 0.6 copy.30
  124.0 0.6 copy.31
  124.6 0.6 copy.32
  125.3 0.6 copy.33
  (2 shorter events, 0.0 us)
Async XLA Ops:
  2.1 1.6 %copy-start = (bf16[1024,1024]{1,0:T(8,128)(2,1)S(1)}, bf16[1024,1024]{1,0:T(8,128)(2,1)}, u32[]{:S(2)}) copy-start(bf16[1024,1024]{1,0:T(8,128)(2,1)} %a_in.1) | copy-start | bytes 6291460
  3.7 1.0 copy-start.1
  4.7 0.8 copy-start.2
  5.6 0.8 copy-start.3
  6.4 0.8 copy-start.4
  7.2 0.8 copy-start.5
  8.0 0.8 copy-start.6
  8.8 0.7 copy-start.7

commit v2 on v1

--- a/solution.py
+++ b/solution.py
@@ -13,7 +13,8 @@
 FAC = 64
 PIECES = 4
 SKEW = 2
-AHEAD = 2
+AHEAD = 4
+VMEM_BYTES = 62 * 1024 * 1024
 
 adapter_scale = 2.0
 beta_one = 0.9
@@ -26,15 +27,18 @@
 BF16 = jnp.bfloat16
 MESH = pl.DeviceIdType.MESH
 
-AT_FORWARD = 1
-AT_PROJECT = 3
-AT_STRIPE_SUM = 5
-AT_TENSOR_SUM = 6
-AT_STRIPE_SPREAD = 8
-AT_GRADIENT = 9
-AT_GROUP_SUM = 12
-AT_HALF_SUM = 15
-AT_UP_ADAM = 17
+AT_GREET = 0
+AT_EXCHANGE = 4
+AT_FORWARD = 7
+AT_PROJECT = 9
+AT_STRIPE_SUM = 11
+AT_TENSOR_SUM = 13
+AT_STRIPE_SPREAD = 15
+AT_GRADIENT = 17
+AT_ADAPTER = 19
+AT_GROUP_SUM = 21
+AT_HALF_SUM = 24
+AT_UP_ADAM = 26
 
 
 def adam(params, moment, second, gradient):
@@ -59,7 +63,7 @@
     line_send, line_recv,
     fac_send, fac_recv,
     xr_send, xr_recv, zr_send, zr_recv, za_send, za_recv, xa_send, xa_recv,
-    gr_send, gr_recv, gz_send, gz_recv, ux_send, ux_recv,
+    gr_send, gr_recv, gz_send, gz_recv, ux_send, ux_recv, hello,
 ):
     G = NP // 2
     TOK, C = av.shape
@@ -112,13 +116,20 @@
     for load in loads[3:]:
         load.start()
 
+    z = zh * NT + t
+    after = {"dp": jnp.where(t == NT - 1, p + G, p), "tensor": lax.rem(t + 1, NT)}
+    before = {"dp": jnp.where(t == 0, p - G, p), "tensor": lax.rem(t + NT - 1, NT)}
+    has_after, has_before = z < 2 * NT - 1, z > 0
     barrier = pltpu.get_barrier_semaphore()
-    partners = [other("tensor", t, NT, o) for o in range(1, NT)]
-    partners += [other("stripe", s, S, o) for o in range(1, S)]
+    partners = [other("stripe", s, S, o) for o in range(1, S)]
     partners += [{"dp": group_peer(o)} for o in range(1, G)]
-    partners += [{"dp": pz}]
     for partner in partners:
         pl.semaphore_signal(barrier, inc=1, device_id=partner, device_id_type=MESH)
+    for there, partner in ((has_after, after), (has_before, before)):
+
+        @pl.when(there)
+        def _(partner=partner):
+            pl.semaphore_signal(barrier, inc=1, device_id=partner, device_id_type=MESH)
 
     loads[2].wait()
 
@@ -127,11 +138,41 @@
         rows = pl.ds(pl.multiple_of(b * BLK, BLK), BLK)
         place = lax.broadcasted_iota(jnp.int32, (BLK, C), 0)
         block = av[rows, :]
-        av[rows, :] = jnp.where(place < fill_ref[b, 0], block, jnp.zeros_like(block))
+        av[rows, :] = jnp.where(place < fill_ref[0, b], block, jnp.zeros_like(block))
+
+    def multiply(i):
+        j = order(i)
+        w_load(j).wait()
+        part = lax.dot_general(
+            av[...],
+            wv[pl.ds(pl.multiple_of(j * CHUNK, CHUNK), CHUNK), :],
+            (((1,), (1,)), ((), ())),
+            preferred_element_type=F32,
+        )
+        pv[j] = part.astype(BF16)
+
+    multiply(jnp.int32(0))
 
     loads[0].wait()
     loads[1].wait()
-    pl.semaphore_wait(barrier, len(partners))
+    pl.semaphore_wait(barrier, len(partners) + jnp.where(has_after & has_before, 2, 1))
+
+    def greet(slot):
+        for way, to, there in ((0, after, has_after), (1, before, has_before)):
+            r = z if way == 0 else 2 * NT - 1 - z
+            if slot >= 1:
+
+                @pl.when(r >= slot + 1)
+                def _(way=way):
+                    pl.semaphore_wait(hello.at[way, slot], 1)
+
+            if slot + 1 < NT:
+
+                @pl.when((r >= slot + 1) & there)
+                def _(way=way, to=to):
+                    pl.semaphore_signal(hello.at[way, slot + 1], inc=1, device_id=to, device_id_type=MESH)
+
+    greet(0)
 
     def remote(src, dst, send, recv, device):
         return pltpu.make_async_remote_copy(
@@ -173,9 +214,11 @@
     def ux_copy(o):
         return remote(ux.at[s], ux.at[s], ux_send.at[o], ux_recv.at[s], other("stripe", s, S, o))
 
-    fac_copy(p, 0, {"dp": pz}).start()
     for o in range(1, G):
         fac_copy(p, o, {"dp": group_peer(o)}).start()
+
+    def exchange():
+        fac_copy(p, 0, {"dp": pz}).start()
 
     def forward():
         fac_copy(pz, 0, {"dp": pz}).wait_recv()
@@ -193,7 +236,7 @@
         @pl.loop(0, NB)
         def _(b):
             rows = pl.ds(pl.multiple_of(b * BLK, BLK), BLK)
-            chosen = fac[ten_ref[b, 0]]
+            chosen = fac[ten_ref[0, b]]
             nt = (((1,), (1,)), ((), ()))
             low = lax.dot_general(chosen[:DOWN], xv[rows, :], nt, preferred_element_type=F32)
             grad = av[rows, quarter]
@@ -263,7 +306,7 @@
         block_of = lax.div(lax.broadcasted_iota(jnp.int32, (1, TOK), 1), BLK)
         tenant = jnp.zeros((1, TOK), jnp.int32)
         for b in range(NB):
-            tenant = jnp.where(block_of == b, ten_ref[b, 0], tenant)
+            tenant = jnp.where(block_of == b, ten_ref[0, b], tenant)
         last = s == S - 1
         sec_first = jnp.where(last, RANK, 0)
         sec_second = jnp.where(last, 2 * RANK, 0)
@@ -293,10 +336,11 @@
         for o in range(1, G):
             gr_copy(o).start()
 
+    def adapter():
         @pl.loop(0, NB)
         def _(b):
             rows = pl.ds(pl.multiple_of(b * BLK, BLK), BLK)
-            down = fac[ten_ref[b, 0]][:DOWN]
+            down = fac[ten_ref[0, b]][:DOWN]
             extra = lax.dot_general(
                 lb[pl.ds(DOWN, DOWN), rows], down, (((0,), (0,)), ((), ())), preferred_element_type=F32
             )
@@ -350,21 +394,6 @@
         pltpu.make_async_copy(uvv, uv_o.at[0], store_sem.at[5]),
     ]
 
-    def multiply(i):
-        j = order(i)
-        w_load(j).wait()
-
-        @pl.loop(0, PIECES)
-        def _(q):
-            rows = pl.ds(pl.multiple_of(q * PR, PR), PR)
-            part = lax.dot_general(
-                av[rows, :],
-                wv[pl.ds(pl.multiple_of(j * CHUNK, CHUNK), CHUNK), :],
-                (((1,), (1,)), ((), ())),
-                preferred_element_type=F32,
-            )
-            pv[j, rows, :] = part.astype(BF16)
-
     def rank(way):
         return t if way == 0 else NT - 1 - t
 
@@ -397,13 +426,17 @@
 
                 copy.start()
 
-    stages = [
+    greetings = range(1, NT)
+    stages = [(AT_GREET + (slot + 0) // 2, functools.partial(greet, slot)) for slot in greetings]
+    stages += [
+        (AT_EXCHANGE, exchange),
         (AT_FORWARD, forward),
         (AT_PROJECT, project),
         (AT_STRIPE_SUM, stripe_sum),
         (AT_TENSOR_SUM, tensor_sum),
         (AT_STRIPE_SPREAD, stripe_spread),
         (AT_GRADIENT, gradient),
+        (AT_ADAPTER, adapter),
         (AT_GROUP_SUM, group_sum),
         (AT_HALF_SUM, half_sum),
         (AT_UP_ADAM, up_adam),
@@ -413,11 +446,12 @@
 
     @pl.loop(0, steps)
     def _(v):
-        @pl.when(v < NT)
+        line_step(v)
+
+        @pl.when(v < NT - 1)
         def _():
-            multiply(v)
-
-        line_step(v)
+            multiply(v + 1)
+
         for at, stage in stages:
             pl.when(v == at)(stage)
 
@@ -471,6 +505,19 @@
     gz_copy().wait_send()
     for store in stores:
         store.wait()
+    for write in writes:
+        write.wait()
+
+
+def deliver(*refs):
+    ins, outs, held, (sems,) = refs[:7], refs[7:14], refs[14:21], refs[21:]
+    copies = [pltpu.make_async_copy(ins[i], held[i], sems.at[i]) for i in range(7)]
+    for copy in copies:
+        copy.start()
+    writes = [pltpu.make_async_copy(held[i], outs[i], sems.at[7 + i]) for i in range(7)]
+    for copy, write in zip(copies, writes):
+        copy.wait()
+        write.start()
     for write in writes:
         write.wait()
 
@@ -495,6 +542,7 @@
     G = NP // 2
     qt = tok // S
     any_space = pl.BlockSpec(memory_space=pl.ANY)
+    hbm = pl.BlockSpec(memory_space=pltpu.HBM)
     smem = pl.BlockSpec(memory_space=pltpu.SMEM)
     outs = (
         jax.ShapeDtypeStruct((tok, d), BF16),
@@ -539,24 +587,24 @@
         dma((NT, PIECES)), dma((2, NT, PIECES)),
         dma((2 * G,)), dma((NP,)),
         dma((S,)), dma((S,)), dma((6,)), dma((6, NT)), dma((6, NT)), dma((6,)), dma((S,)), dma((S,)),
-        dma((G,)), dma((G,)), dma, dma, dma((S,)), dma((S,)),
+        dma((G,)), dma((G,)), dma, dma, dma((S,)), dma((S,)), pltpu.SemaphoreType.REGULAR((2, NT)),
     ]
-    return pl.pallas_call(
+    results = pl.pallas_call(
         functools.partial(kernel, S, NP, NT),
         out_shape=outs,
-        in_specs=[smem] * 2 + [any_space] * 9,
+        in_specs=[smem] * 2 + [hbm] * 9,
         out_specs=[any_space] * 7,
         scratch_shapes=scratch,
         compiler_params=pltpu.CompilerParams(
-            collective_id=0, has_side_effects=True, vmem_limit_bytes=48 * 1024 * 1024
+            collective_id=0, has_side_effects=True, vmem_limit_bytes=VMEM_BYTES
         ),
         cost_estimate=pl.CostEstimate(
             flops=2 * tok * c * w_rows, bytes_accessed=2 * (tok * c + w_rows * c), transcendentals=0
         ),
         name="united_backward",
     )(
-        block_owner_tenant,
-        block_token_fill,
+        block_owner_tenant.T,
+        block_token_fill.T,
         normed_layer_input,
         projection_output_gradient,
         frozen_projection_weight,
@@ -567,6 +615,15 @@
         up_first_moment,
         up_second_moment,
     )
+    return pl.pallas_call(
+        deliver,
+        out_shape=outs,
+        in_specs=[any_space] * 7,
+        out_specs=[hbm] * 7,
+        scratch_shapes=[vm(out.shape, out.dtype) for out in outs] + [dma((14,))],
+        compiler_params=pltpu.CompilerParams(vmem_limit_bytes=VMEM_BYTES),
+        name="deliver",
+    )(*results)
 
 
 def solution(mesh):

time: 126 us -> 106 us (0.84)
  local copies, waits for them, and re-layouts: 13.4 us -> 0 us
  Pallas kernels: 112 us -> 105 us
    unnamed x25 -> x0, local copies, waits for them, and re-layouts: 13.4 us -> none
    pallas_call x1, Pallas kernels: 112 us -> 103 us  [on_device(): pl.pallas_call(functools.partial(kernel, S, NP, NT), out_shape=outs, in_s...]
    pallas_call x0 -> x1, Pallas kernels: none -> 2.04 us  [on_device(): pl.pallas_call(deliver, out_shape=outs, in_specs=[any_space] * 7, out_spe...]
where the time goes in v2:
time: 106 us
  Pallas kernels  105 us (99%)
    pallas_call x1, Pallas kernels, on_device(): pl.pallas_call(functools.partial(kernel, S, NP, NT), out_shape=outs, in_s...  103 us

profile of v2, /device:TPU:32, one launch (start us, length us, event | category | flops | bytes accessed | tf_op | source)
XLA Modules:
  0.0 106.0 jit_solution(4286240023757464540)
XLA Ops:
  0.6 103.3 %united_backward.1 = (bf16[1024,256]{1,0:T(8,128)(2,1)}, bf16[1,48,256]{2,1,0:T(8,128)(2,1)}, f32[1,48,256]{2,1,0:T(8,128)}, f32[1,48,256]{2,1,0:T(8,128)}, bf16...) custom-call(s32[1,8]{1,0:T(1,128)} %bitcast.2, s32[1,8]{1,0:T(1,128)} %bitcast.3, ...), custom_call_target="tpu_custom_call" | custom-call | flops 4294967296 | bytes 6291456 | tf_op jit(solution)/shard_map/united_backward/pallas_call | solution.py:592
  103.9 2.0 %deliver.1 = (bf16[1024,256]{1,0:T(8,128)(2,1)}, bf16[1,48,256]{2,1,0:T(8,128)(2,1)}, f32[1,48,256]{2,1,0:T(8,128)}, f32[1,48,256]{2,1,0:T(8,128)}, bf16[1,16,10...) custom-call(bf16[1024,256]{1,0:T(8,128)(2,1)} %get-tuple-element.14.refs_0_, ...), custom_call_target="tpu_custom_call" | custom-call | tf_op jit(solution)/shard_map/deliver/pallas_call | solution.py:618

commit v3 on v2

--- a/solution.py
+++ b/solution.py
@@ -28,17 +28,20 @@
 MESH = pl.DeviceIdType.MESH
 
 AT_GREET = 0
-AT_EXCHANGE = 4
-AT_FORWARD = 7
-AT_PROJECT = 9
-AT_STRIPE_SUM = 11
-AT_TENSOR_SUM = 13
+AT_EXCHANGE = 1
+AT_RELAY = 3
+AT_FORWARD = 5
+AT_PROJECT = 8
+AT_STRIPE_SUM = 10
+AT_TENSOR_SUM = 12
 AT_STRIPE_SPREAD = 15
 AT_GRADIENT = 17
-AT_ADAPTER = 19
-AT_GROUP_SUM = 21
-AT_HALF_SUM = 24
-AT_UP_ADAM = 26
+AT_ADAPTER = 18
+AT_GROUP_SUM = 20
+AT_OWN_SUM = 21
+AT_RELAY_SUM = 22
+AT_HALF_SUM = 25
+AT_UP_ADAM = 27
 
 
 def adam(params, moment, second, gradient):
@@ -56,14 +59,15 @@
     x_in, a_in, w_in, dn_in, dm_in, dv_in, up_in, um_in, uv_in,
     out_o, dn_o, dm_o, dv_o, up_o, um_o, uv_o,
     av, wv, xv, fac, pv, rv,
-    lp, xrs, xs, zrs, lb,
+    lp, xrs, xs, zrs, lb, fac_held, sum_held,
     gl, ul, gp, grs, go, gs, gz, ux, acc, ov,
     dmv, dvv, umv, uvv, upv, dnn, upn,
-    load_sem, w_sem, out_sem, store_sem,
+    load_sem, a_sem, w_sem, out_sem, store_sem,
     line_send, line_recv,
     fac_send, fac_recv,
     xr_send, xr_recv, zr_send, zr_recv, za_send, za_recv, xa_send, xa_recv,
     gr_send, gr_recv, gz_send, gz_recv, ux_send, ux_recv, hello,
+    out_send, relay_send, relay_recv,
 ):
     G = NP // 2
     TOK, C = av.shape
@@ -81,6 +85,11 @@
     m = lax.rem(p, G)
     pz = (1 - zh) * G + m
 
+    def remote(src, dst, send, recv, device):
+        return pltpu.make_async_remote_copy(
+            src_ref=src, dst_ref=dst, send_sem=send, recv_sem=recv, device_id=device, device_id_type=MESH
+        )
+
     def other(axis, here, size, o):
         return {axis: lax.rem(here + o, size)}
 
@@ -92,13 +101,12 @@
     loads = [
         pltpu.make_async_copy(dn_in.at[0], fac.at[p, pl.ds(0, DOWN)], load_sem.at[0]),
         pltpu.make_async_copy(up_in.at[0, :, quarter], fac.at[p, pl.ds(DOWN, RANK)], load_sem.at[1]),
-        pltpu.make_async_copy(a_in, av, load_sem.at[2]),
-        pltpu.make_async_copy(x_in, xv, load_sem.at[3]),
-        pltpu.make_async_copy(dm_in.at[0], dmv, load_sem.at[4]),
-        pltpu.make_async_copy(dv_in.at[0], dvv, load_sem.at[5]),
-        pltpu.make_async_copy(um_in.at[0], umv, load_sem.at[6]),
-        pltpu.make_async_copy(uv_in.at[0], uvv, load_sem.at[7]),
-        pltpu.make_async_copy(up_in.at[0], upv, load_sem.at[8]),
+        pltpu.make_async_copy(x_in, xv, load_sem.at[2]),
+        pltpu.make_async_copy(dm_in.at[0], dmv, load_sem.at[3]),
+        pltpu.make_async_copy(dv_in.at[0], dvv, load_sem.at[4]),
+        pltpu.make_async_copy(um_in.at[0], umv, load_sem.at[5]),
+        pltpu.make_async_copy(uv_in.at[0], uvv, load_sem.at[6]),
+        pltpu.make_async_copy(up_in.at[0], upv, load_sem.at[7]),
     ]
 
     def order(i):
@@ -109,11 +117,19 @@
         rows = pl.ds(pl.multiple_of(j * CHUNK, CHUNK), CHUNK)
         return pltpu.make_async_copy(w_in.at[rows], wv.at[rows], w_sem.at[j])
 
-    for load in loads[:3]:
+    def a_load(q):
+        rows = pl.ds(q * PR, PR)
+        return pltpu.make_async_copy(a_in.at[rows], av.at[rows], a_sem.at[q])
+
+    a_load(0).start()
+    w_load(order(jnp.int32(0))).start()
+    for load in loads[:2]:
         load.start()
-    for i in range(NT):
+    for q in range(1, PIECES):
+        a_load(q).start()
+    for i in range(1, NT):
         w_load(order(jnp.int32(i))).start()
-    for load in loads[3:]:
+    for load in loads[2:]:
         load.start()
 
     z = zh * NT + t
@@ -131,15 +147,6 @@
         def _(partner=partner):
             pl.semaphore_signal(barrier, inc=1, device_id=partner, device_id_type=MESH)
 
-    loads[2].wait()
-
-    @pl.loop(0, NB)
-    def _(b):
-        rows = pl.ds(pl.multiple_of(b * BLK, BLK), BLK)
-        place = lax.broadcasted_iota(jnp.int32, (BLK, C), 0)
-        block = av[rows, :]
-        av[rows, :] = jnp.where(place < fill_ref[0, b], block, jnp.zeros_like(block))
-
     def multiply(i):
         j = order(i)
         w_load(j).wait()
@@ -151,8 +158,29 @@
         )
         pv[j] = part.astype(BF16)
 
-    multiply(jnp.int32(0))
-
+    def begin(q):
+        a_load(q).wait()
+
+        @pl.loop(q * PR // BLK, (q + 1) * PR // BLK)
+        def _(b):
+            rows = pl.ds(pl.multiple_of(b * BLK, BLK), BLK)
+            place = lax.broadcasted_iota(jnp.int32, (BLK, C), 0)
+            block = av[rows, :]
+            av[rows, :] = jnp.where(place < fill_ref[0, b], block, jnp.zeros_like(block))
+
+        j = order(jnp.int32(0))
+        if q == 0:
+            w_load(j).wait()
+        rows = pl.ds(q * PR, PR)
+        part = lax.dot_general(
+            av[rows, :],
+            wv[pl.ds(pl.multiple_of(j * CHUNK, CHUNK), CHUNK), :],
+            (((1,), (1,)), ((), ())),
+            preferred_element_type=F32,
+        )
+        pv[j, rows, :] = part.astype(BF16)
+
+    begin(0)
     loads[0].wait()
     loads[1].wait()
     pl.semaphore_wait(barrier, len(partners) + jnp.where(has_after & has_before, 2, 1))
@@ -166,18 +194,46 @@
                 def _(way=way):
                     pl.semaphore_wait(hello.at[way, slot], 1)
 
-            if slot + 1 < NT:
+            if slot + 1 < NT - 1:
 
                 @pl.when((r >= slot + 1) & there)
                 def _(way=way, to=to):
                     pl.semaphore_signal(hello.at[way, slot + 1], inc=1, device_id=to, device_id_type=MESH)
 
+    def rank(way):
+        return t if way == 0 else NT - 1 - t
+
+    def line_copy(way, u):
+        k, q = lax.div(u, PIECES), lax.rem(u, PIECES)
+        j = NT - 1 - k if way == 0 else k
+        rows = pl.ds(pl.multiple_of(q * PR, PR), PR)
+        to = t + 1 if way == 0 else t - 1
+        return j, rows, remote(
+            pv.at[j, rows], rv.at[way, j, rows], line_send.at[j, q], line_recv.at[way, j, q], {"tensor": to}
+        )
+
+    def line_step(v):
+        for way in range(2):
+            r = rank(way)
+            u = v - SKEW * r
+
+            @pl.when((u >= 0) & (u < (NT - 1 - r) * PIECES))
+            def _(way=way, r=r, u=u):
+                j, rows, copy = line_copy(way, u)
+
+                @pl.when(r > 0)
+                def _():
+                    copy.wait_recv()
+                    pv[j, rows, :] = (pv[j, rows, :].astype(F32) + rv[way, j, rows, :].astype(F32)).astype(BF16)
+
+                @pl.when(u >= AHEAD)
+                def _():
+                    line_copy(way, u - AHEAD)[2].wait_send()
+
+                copy.start()
+
     greet(0)
-
-    def remote(src, dst, send, recv, device):
-        return pltpu.make_async_remote_copy(
-            src_ref=src, dst_ref=dst, send_sem=send, recv_sem=recv, device_id=device, device_id_type=MESH
-        )
+    line_step(jnp.int32(0))
 
     def fac_copy(slot, i, device):
         return remote(fac.at[slot], fac.at[slot], fac_send.at[i], fac_recv.at[slot], device)
@@ -204,12 +260,31 @@
         part = lb.at[:, my_tokens]
         return remote(part, part, xa_send.at[o], xa_recv.at[s], other("stripe", s, S, o))
 
-    def gr_copy(o):
+    def gr_copy(o, half):
         to = lax.rem(m + o, G)
-        return remote(gp.at[to], grs.at[m], gr_send.at[o], gr_recv.at[m], {"dp": zh * G + to})
-
-    def gz_copy():
-        return remote(gs, gz, gz_send, gz_recv, {"dp": pz})
+        return remote(
+            gp.at[to, half], grs.at[m, half], gr_send.at[o, half], gr_recv.at[m, half], {"dp": zh * G + to}
+        )
+
+    MID = NT // 2
+    far = lax.rem(t + MID, NT)
+    half_way = {"dp": jnp.where(t < MID, m, G + m), "tensor": far}
+    is_relay = (z >= MID) & (z < NT + MID)
+
+    def to_relay(src, buf, i):
+        return remote(src, buf.at[zh], out_send.at[i], relay_recv.at[i, zh], half_way)
+
+    def from_relay(buf, dst, i, side, recv):
+        return remote(
+            buf.at[side], dst, relay_send.at[i, side], recv, {"dp": (1 - side) * G + m, "tensor": far}
+        )
+
+    def fac_relay(side):
+        slot = side * G + m
+        return from_relay(fac_held, fac.at[slot], 0, side, fac_recv.at[slot])
+
+    def sum_relay(side):
+        return from_relay(sum_held, gz, 1, side, gz_recv)
 
     def ux_copy(o):
         return remote(ux.at[s], ux.at[s], ux_send.at[o], ux_recv.at[s], other("stripe", s, S, o))
@@ -217,8 +292,26 @@
     for o in range(1, G):
         fac_copy(p, o, {"dp": group_peer(o)}).start()
 
+    for q in range(1, PIECES):
+        begin(q)
+    greet(1)
+
     def exchange():
-        fac_copy(p, 0, {"dp": pz}).start()
+        to_relay(fac.at[p], fac_held, 0).start()
+
+    def relay():
+        @pl.when(is_relay)
+        def _():
+            for side in range(2):
+                remote(gs, fac_held.at[side], gz_send, relay_recv.at[0, side], {"dp": pz}).wait_recv()
+                fac_relay(side).start()
+
+    def relay_sum():
+        @pl.when(is_relay)
+        def _():
+            for side in range(2):
+                remote(gs, sum_held.at[side], gz_send, relay_recv.at[1, side], {"dp": pz}).wait_recv()
+                sum_relay(side).start()
 
     def forward():
         fac_copy(pz, 0, {"dp": pz}).wait_recv()
@@ -229,7 +322,7 @@
         for o in range(1, G):
             fac_copy(zh * G + lax.rem(m + o, G), 0, {"dp": pz}).wait_recv()
             fac_copy((1 - zh) * G + lax.rem(m + o, G), 0, {"dp": pz}).wait_recv()
-        loads[3].wait()
+        loads[2].wait()
         last = s == S - 1
         zero = jnp.zeros((RANK, BLK), F32)
 
@@ -333,8 +426,9 @@
             for n in range(NP):
                 gp[n % G, n // G, DOWN:, h * HALF : (h + 1) * HALF] = part[n * RANK : (n + 1) * RANK]
 
-        for o in range(1, G):
-            gr_copy(o).start()
+        for half in (1 - zh, zh):
+            for o in range(1, G):
+                gr_copy(o, half).start()
 
     def adapter():
         @pl.loop(0, NB)
@@ -346,28 +440,30 @@
             )
             acc[rows, :] = extra + pv[t, rows, :].astype(F32)
 
-    def group_sum():
+    def total(half):
+        value = gp[m, half].astype(F32)
         for o in range(1, G):
             src = lax.rem(m + o, G)
-            remote(gp.at[0], grs.at[src], gr_send.at[0], gr_recv.at[src], {"dp": pz}).wait_recv()
-
-        def total(half):
-            value = gp[m, half].astype(F32)
-            for o in range(1, G):
-                value += grs[lax.rem(m + o, G), half].astype(F32)
-            return value
-
+            remote(
+                gp.at[0, half], grs.at[src, half], gr_send.at[0, half], gr_recv.at[src, half], {"dp": pz}
+            ).wait_recv()
+            value += grs[src, half].astype(F32)
+        return value
+
+    def group_sum():
         gs[...] = total(1 - zh).astype(BF16)
-        gz_copy().start()
+        to_relay(gs, sum_held, 1).start()
+
+    def own_sum():
         go[...] = total(zh)
 
     def half_sum():
-        gz_copy().wait_recv()
+        remote(gs, gz, gz_send, gz_recv, {"dp": pz}).wait_recv()
         grad = go[...] + gz[...].astype(F32)
         ux[s] = grad[DOWN:]
         for o in range(1, S):
             ux_copy(o).start()
-        for load in loads[4:]:
+        for load in loads[3:]:
             load.wait()
         dnn[...], dmv[...], dvv[...] = adam(fac[p, :DOWN, :], dmv[...], dvv[...], grad[:DOWN])
         for store in stores[:3]:
@@ -394,42 +490,11 @@
         pltpu.make_async_copy(uvv, uv_o.at[0], store_sem.at[5]),
     ]
 
-    def rank(way):
-        return t if way == 0 else NT - 1 - t
-
-    def line_copy(way, u):
-        k, q = lax.div(u, PIECES), lax.rem(u, PIECES)
-        j = NT - 1 - k if way == 0 else k
-        rows = pl.ds(pl.multiple_of(q * PR, PR), PR)
-        to = t + 1 if way == 0 else t - 1
-        return j, rows, remote(
-            pv.at[j, rows], rv.at[way, j, rows], line_send.at[j, q], line_recv.at[way, j, q], {"tensor": to}
-        )
-
-    def line_step(v):
-        for way in range(2):
-            r = rank(way)
-            u = v - SKEW * r
-
-            @pl.when((u >= 0) & (u < (NT - 1 - r) * PIECES))
-            def _(way=way, r=r, u=u):
-                j, rows, copy = line_copy(way, u)
-
-                @pl.when(r > 0)
-                def _():
-                    copy.wait_recv()
-                    pv[j, rows, :] = (pv[j, rows, :].astype(F32) + rv[way, j, rows, :].astype(F32)).astype(BF16)
-
-                @pl.when(u >= AHEAD)
-                def _():
-                    line_copy(way, u - AHEAD)[2].wait_send()
-
-                copy.start()
-
-    greetings = range(1, NT)
-    stages = [(AT_GREET + (slot + 0) // 2, functools.partial(greet, slot)) for slot in greetings]
+    greetings = range(2, NT - 1)
+    stages = [(AT_GREET + slot // 2, functools.partial(greet, slot)) for slot in greetings]
     stages += [
         (AT_EXCHANGE, exchange),
+        (AT_RELAY, relay),
         (AT_FORWARD, forward),
         (AT_PROJECT, project),
         (AT_STRIPE_SUM, stripe_sum),
@@ -438,19 +503,21 @@
         (AT_GRADIENT, gradient),
         (AT_ADAPTER, adapter),
         (AT_GROUP_SUM, group_sum),
+        (AT_OWN_SUM, own_sum),
+        (AT_RELAY_SUM, relay_sum),
         (AT_HALF_SUM, half_sum),
         (AT_UP_ADAM, up_adam),
     ]
     steps = max((NT - 1 - r) * PIECES + SKEW * r for r in range(NT - 1))
     steps = max(steps, AT_UP_ADAM + 1, NT)
 
-    @pl.loop(0, steps)
+    @pl.loop(1, steps)
     def _(v):
         line_step(v)
 
-        @pl.when(v < NT - 1)
+        @pl.when(v < NT)
         def _():
-            multiply(v + 1)
+            multiply(v)
 
         for at, stage in stages:
             pl.when(v == at)(stage)
@@ -482,11 +549,11 @@
             for back in range(AHEAD):
                 line_copy(way, (NT - 1 - r) * PIECES - AHEAD + back)[2].wait_send()
 
-    fac_copy(p, 0, {"dp": pz}).wait_send()
     for o in range(1, G):
         fac_copy(p, o, {"dp": group_peer(o)}).wait_send()
         fac_copy(pz, G + o, {"dp": group_peer(o)}).wait_send()
-        gr_copy(o).wait_send()
+        gr_copy(o, 0).wait_send()
+        gr_copy(o, 1).wait_send()
     for o in range(1, S):
         xr_copy(o).wait_send()
         xa_copy(o).wait_send()
@@ -502,7 +569,15 @@
             for o in range(1, NT):
                 za_copy(g, o).wait_send()
 
-    gz_copy().wait_send()
+    to_relay(fac.at[p], fac_held, 0).wait_send()
+    to_relay(gs, sum_held, 1).wait_send()
+
+    @pl.when(is_relay)
+    def _():
+        for side in range(2):
+            fac_relay(side).wait_send()
+            sum_relay(side).wait_send()
+
     for store in stores:
         store.wait()
     for write in writes:
@@ -566,6 +641,8 @@
         vm((2 * DOWN, qt), BF16),
         vm((6, NT, RANK, qt), BF16),
         vm((2 * DOWN, tok), BF16),
+        vm((2, FAC, d), BF16),
+        vm((2, FAC, d), BF16),
         vm((NP * DOWN, tok), BF16),
         vm((2, NP * RANK, tok), BF16),
         vm((G, 2, FAC, d), BF16),
@@ -583,11 +660,12 @@
         vm((RANK, c), BF16),
         vm((DOWN, d), BF16),
         vm((RANK, c), BF16),
-        dma((9,)), dma((NT,)), dma((PIECES,)), dma((6,)),
+        dma((8,)), dma((PIECES,)), dma((NT,)), dma((PIECES,)), dma((6,)),
         dma((NT, PIECES)), dma((2, NT, PIECES)),
         dma((2 * G,)), dma((NP,)),
         dma((S,)), dma((S,)), dma((6,)), dma((6, NT)), dma((6, NT)), dma((6,)), dma((S,)), dma((S,)),
-        dma((G,)), dma((G,)), dma, dma, dma((S,)), dma((S,)), pltpu.SemaphoreType.REGULAR((2, NT)),
+        dma((G, 2)), dma((G, 2)), dma, dma, dma((S,)), dma((S,)), pltpu.SemaphoreType.REGULAR((2, NT)),
+        dma((2,)), dma((2, 2)), dma((2, 2)),
     ]
     results = pl.pallas_call(
         functools.partial(kernel, S, NP, NT),

time: 106 us -> 104 us (0.981)
  the two profiles are of different devices: /device:TPU:32 before, /device:TPU:196 now
where the time goes in v3:
time: 104 us
  Pallas kernels  103 us (99%)
    pallas_call x1, Pallas kernels, on_device(): pl.pallas_call(functools.partial(kernel, S, NP, NT), out_shape=outs, in_s...  101 us

profile of v3, /device:TPU:196, one launch (start us, length us, event | category | flops | bytes accessed | tf_op | source)
XLA Modules:
  0.0 103.7 jit_solution(13269924964853796974)
XLA Ops:
  0.6 101.0 %united_backward.1 = (bf16[1024,256]{1,0:T(8,128)(2,1)}, bf16[1,48,256]{2,1,0:T(8,128)(2,1)}, f32[1,48,256]{2,1,0:T(8,128)}, f32[1,48,256]{2,1,0:T(8,128)}, bf16...) custom-call(s32[1,8]{1,0:T(1,128)} %bitcast.2, s32[1,8]{1,0:T(1,128)} %bitcast.3, ...), custom_call_target="tpu_custom_call" | custom-call | flops 4294967296 | bytes 6291456 | tf_op jit(solution)/shard_map/united_backward/pallas_call | solution.py:670
  101.7 2.0 %deliver.1 = (bf16[1024,256]{1,0:T(8,128)(2,1)}, bf16[1,48,256]{2,1,0:T(8,128)(2,1)}, f32[1,48,256]{2,1,0:T(8,128)}, f32[1,48,256]{2,1,0:T(8,128)}, bf16[1,16,10...) custom-call(bf16[1024,256]{1,0:T(8,128)(2,1)} %get-tuple-element.14.refs_0_, ...), custom_call_target="tpu_custom_call" | custom-call | tf_op jit(solution)/shard_map/deliver/pallas_call | solution.py:696

commit v4 on v3

--- a/solution.py
+++ b/solution.py
@@ -194,7 +194,7 @@
                 def _(way=way):
                     pl.semaphore_wait(hello.at[way, slot], 1)
 
-            if slot + 1 < NT - 1:
+            if slot + 1 < NT:
 
                 @pl.when((r >= slot + 1) & there)
                 def _(way=way, to=to):
@@ -283,8 +283,8 @@
         slot = side * G + m
         return from_relay(fac_held, fac.at[slot], 0, side, fac_recv.at[slot])
 
-    def sum_relay(side):
-        return from_relay(sum_held, gz, 1, side, gz_recv)
+    def gz_copy():
+        return remote(gs, gz, gz_send, gz_recv, {"dp": pz})
 
     def ux_copy(o):
         return remote(ux.at[s], ux.at[s], ux_send.at[o], ux_recv.at[s], other("stripe", s, S, o))
@@ -305,13 +305,6 @@
             for side in range(2):
                 remote(gs, fac_held.at[side], gz_send, relay_recv.at[0, side], {"dp": pz}).wait_recv()
                 fac_relay(side).start()
-
-    def relay_sum():
-        @pl.when(is_relay)
-        def _():
-            for side in range(2):
-                remote(gs, sum_held.at[side], gz_send, relay_recv.at[1, side], {"dp": pz}).wait_recv()
-                sum_relay(side).start()
 
     def forward():
         fac_copy(pz, 0, {"dp": pz}).wait_recv()
@@ -452,13 +445,13 @@
 
     def group_sum():
         gs[...] = total(1 - zh).astype(BF16)
-        to_relay(gs, sum_held, 1).start()
+        gz_copy().start()
 
     def own_sum():
         go[...] = total(zh)
 
     def half_sum():
-        remote(gs, gz, gz_send, gz_recv, {"dp": pz}).wait_recv()
+        gz_copy().wait_recv()
         grad = go[...] + gz[...].astype(F32)
         ux[s] = grad[DOWN:]
         for o in range(1, S):
@@ -490,8 +483,8 @@
         pltpu.make_async_copy(uvv, uv_o.at[0], store_sem.at[5]),
     ]
 
-    greetings = range(2, NT - 1)
-    stages = [(AT_GREET + slot // 2, functools.partial(greet, slot)) for slot in greetings]
+    greetings = range(2, NT)
+    stages = [(AT_GREET + max(1, slot - 2), functools.partial(greet, slot)) for slot in greetings]
     stages += [
         (AT_EXCHANGE, exchange),
         (AT_RELAY, relay),
@@ -504,7 +497,6 @@
         (AT_ADAPTER, adapter),
         (AT_GROUP_SUM, group_sum),
         (AT_OWN_SUM, own_sum),
-        (AT_RELAY_SUM, relay_sum),
         (AT_HALF_SUM, half_sum),
         (AT_UP_ADAM, up_adam),
     ]
@@ -570,13 +562,12 @@
                 za_copy(g, o).wait_send()
 
     to_relay(fac.at[p], fac_held, 0).wait_send()
-    to_relay(gs, sum_held, 1).wait_send()
+    gz_copy().wait_send()
 
     @pl.when(is_relay)
     def _():
         for side in range(2):
             fac_relay(side).wait_send()
-            sum_relay(side).wait_send()
 
     for store in stores:
         store.wait()

time: 104 us -> 104 us (level)
  the two profiles are of different devices: /device:TPU:196 before, /device:TPU:32 now
where the time goes in v4:
time: 104 us; the launch traced here: 103 us
  Pallas kernels  103 us (99%)
    pallas_call x1, Pallas kernels, on_device(): pl.pallas_call(functools.partial(kernel, S, NP, NT), out_shape=outs, in_s...  101 us

profile of v4, /device:TPU:32, one launch (start us, length us, event | category | flops | bytes accessed | tf_op | source)
XLA Modules:
  0.0 103.5 jit_solution(11339400508742751560)
XLA Ops:
  0.6 100.8 %united_backward.1 = (bf16[1024,256]{1,0:T(8,128)(2,1)}, bf16[1,48,256]{2,1,0:T(8,128)(2,1)}, f32[1,48,256]{2,1,0:T(8,128)}, f32[1,48,256]{2,1,0:T(8,128)}, bf16...) custom-call(s32[1,8]{1,0:T(1,128)} %bitcast.2, s32[1,8]{1,0:T(1,128)} %bitcast.3, ...), custom_call_target="tpu_custom_call" | custom-call | flops 4294967296 | bytes 6291456 | tf_op jit(solution)/shard_map/united_backward/pallas_call | solution.py:661
  101.4 2.0 %deliver.1 = (bf16[1024,256]{1,0:T(8,128)(2,1)}, bf16[1,48,256]{2,1,0:T(8,128)(2,1)}, f32[1,48,256]{2,1,0:T(8,128)}, f32[1,48,256]{2,1,0:T(8,128)}, bf16[1,16,10...) custom-call(bf16[1024,256]{1,0:T(8,128)(2,1)} %get-tuple-element.14.refs_0_, ...), custom_call_target="tpu_custom_call" | custom-call | tf_op jit(solution)/shard_map/deliver/pallas_call | solution.py:687
